TPU v7x, 512 devices: a whole 4x4x16 slice. The times are simulated.
512 devices in a mesh: view: 32 (over x, z_hi, core), seq: 16 (over y, z_lo).
Axes of the slice: x: 4, y: 4, z: 16 (z_hi: 4, z_lo: 4; z = z_hi * 4 + z_lo), core: 2. Of those that a mesh axis runs over, the one named last changes fastest.
Arguments:
- query_rows: bfloat16 [32, 2048, 768], P('view', 'seq'), may hold values from -162 to 162
- key_rows: bfloat16 [32, 2048, 768], P('view', 'seq'), may hold values from -4.5 to 4.5
- value_rows: bfloat16 [32, 2048, 768], P('view', 'seq'), may hold values from -6 to 6
- head_gate: float32 [12], replicated, may hold values from 0.5 to 2
- cotangent: bfloat16 [32, 2048, 768], P('view', 'seq'), may hold values from -80 to 80
- neighbours: int32 [32, 4], P('view'), may hold values from 0 to 31, as said below
- counts: int32 [32], P('view'), may hold values from 1 to 4, as said below
Outputs:
- output: bfloat16 [32, 2048, 768], P('view', 'seq')
- query_grad: bfloat16 [32, 2048, 768], P('view', 'seq')
- key_grad: bfloat16 [32, 2048, 768], P('view', 'seq')
- value_grad: bfloat16 [32, 2048, 768], P('view', 'seq')
- gate_grad: float32 [12], replicated
Inputs may be any that keep to these rules, and one draw needn't show every extreme that they name: Row v holds the views v - 2, v - 1, v + 1, v + 2 modulo 32, each once; the first counts[v] of them are the neighbours of v. Neighbourship is symmetric. `counts`: every view has a neighbour at distance one; some view has four neighbours.
All inputs are finite; a program needn't handle non-finite values.
Results may differ from a plain program's by a relative error of at most 0.035.
Values may be sent and summed in bfloat16 or wider, within the bound.
A program may use at most 64 MiB of HBM per device.

v0:
```python
import math

import jax
import jax.numpy as jnp
from jax import lax
from jax.sharding import PartitionSpec as P


def from_behind(block, axis, distance):
    devices = range(lax.axis_size(axis))
    route = [((i - distance) % len(devices), i) for i in devices]
    return lax.ppermute(block, axis, route)


def rounded_term(term):
    return lax.optimization_barrier(term.astype(jnp.bfloat16))


def shards(query_rows, key_rows, value_rows, head_gate, cotangent, neighbours, counts):
    model_width = query_rows.shape[2]
    head_count = head_gate.shape[0]
    head_size = model_width // head_count
    tokens = query_rows.shape[1]
    score_scale = 1.0 / math.sqrt(head_size)
    view_count = lax.axis_size("view")
    position = lax.axis_index("view")
    offsets = (-2, -1, 1, 2)
    usable = jnp.arange(4) < counts[0]
    present = [
        jnp.any((neighbours[0] == (position + offset) % view_count) & usable) for offset in offsets
    ]
    queries = query_rows[0].reshape(tokens, head_count, head_size)
    own_pair = jnp.concatenate([key_rows[0], value_rows[0]], axis=1)
    arrived = [from_behind(own_pair, "view", -offset) for offset in offsets]
    pair_list = [own_pair] + arrived
    keep_list = [None] + present
    split_pairs = [
        (
            entry[:, :model_width].reshape(tokens, head_count, head_size),
            entry[:, model_width:].reshape(tokens, head_count, head_size),
        )
        for entry in pair_list
    ]

    def masked_scores(row_block, keys_part, keep_flag):
        scores = (
            jnp.einsum("bhd,chd->hbc", row_block, keys_part, preferred_element_type=jnp.float32)
            * score_scale
        )
        if keep_flag is None:
            return scores
        return jnp.where(keep_flag, scores, -jnp.inf)

    first_scores = masked_scores(queries, split_pairs[0][0], None)
    running_max = jnp.max(first_scores, axis=2)
    running_sum = jnp.sum(jnp.exp(first_scores - running_max[:, :, None]), axis=2)
    for index in range(1, 5):
        scores = masked_scores(queries, split_pairs[index][0], keep_list[index])
        new_max = jnp.maximum(running_max, jnp.max(scores, axis=2))
        running_sum = running_sum * jnp.exp(running_max - new_max) + jnp.sum(
            jnp.exp(scores - new_max[:, :, None]), axis=2
        )
        running_max = new_max
    log_total = running_max + jnp.log(running_sum)
    attended = jnp.zeros((tokens, head_count, head_size), jnp.float32)
    for (keys_part, values_part), keep_flag in zip(split_pairs, keep_list):
        weights = jnp.exp(
            masked_scores(queries, keys_part, keep_flag) - log_total[:, :, None]
        ).astype(jnp.bfloat16)
        attended = attended + jnp.einsum(
            "hbc,chd->bhd", weights, values_part, preferred_element_type=jnp.float32
        )
    gate_row = head_gate[None, :, None]
    output = (gate_row * attended).astype(jnp.bfloat16).reshape(1, tokens, model_width)
    cot_view = cotangent[0].reshape(tokens, head_count, head_size).astype(jnp.float32)
    attn_grad = (gate_row * cot_view).astype(jnp.bfloat16)
    row_delta = jnp.transpose(jnp.sum(attn_grad.astype(jnp.float32) * attended, axis=2))
    gate_part = jnp.sum(cot_view * attended, axis=(0, 2))
    gate_sum = lax.psum(gate_part, ("view", "seq"))
    gate_grad = gate_sum / math.sqrt(view_count * lax.axis_size("seq") * tokens * head_size)
    query_acc = jnp.zeros((tokens, head_count, head_size), jnp.float32)
    term_list = []
    for index in range(5):
        keys_part, values_part = split_pairs[index]
        block_scores = masked_scores(queries, keys_part, keep_list[index])
        probs = jnp.exp(block_scores - log_total[:, :, None])
        block_probs_low = probs.astype(jnp.bfloat16)
        prob_grad = jnp.einsum(
            "bhd,chd->hbc", attn_grad, values_part, preferred_element_type=jnp.float32
        )
        block_score_grad = (probs * (prob_grad - row_delta[:, :, None]) * score_scale).astype(
            jnp.bfloat16
        )
        query_acc = query_acc + jnp.einsum(
            "hbc,chd->bhd", block_score_grad, keys_part, preferred_element_type=jnp.float32
        )
        key_term = jnp.einsum(
            "hbc,bhd->chd", block_score_grad, queries, preferred_element_type=jnp.float32
        )
        value_term = jnp.einsum(
            "hbc,bhd->chd", block_probs_low, attn_grad, preferred_element_type=jnp.float32
        )
        joined = jnp.concatenate(
            [key_term.reshape(tokens, model_width), value_term.reshape(tokens, model_width)], axis=1
        )
        term_list.append(rounded_term(joined))
    query_acc, term_list = (query_acc, term_list)
    returned = [from_behind(term, "view", offset) for offset, term in zip(offsets, term_list[1:])]
    total = term_list[0].astype(jnp.float32)
    for term in returned:
        total = total + term.astype(jnp.float32)
    query_grad = query_acc.astype(jnp.bfloat16).reshape(1, tokens, model_width)
    key_grad = total[:, :model_width].astype(jnp.bfloat16).reshape(1, tokens, model_width)
    value_grad = total[:, model_width:].astype(jnp.bfloat16).reshape(1, tokens, model_width)
    return (output, query_grad, key_grad, value_grad, gate_grad)


def solution(mesh):
    in_specs = (
        P("view", "seq", None),
        P("view", "seq", None),
        P("view", "seq", None),
        P(),
        P("view", "seq", None),
        P("view", None),
        P("view"),
    )
    out_specs = (
        P("view", "seq", None),
        P("view", "seq", None),
        P("view", "seq", None),
        P("view", "seq", None),
        P(),
    )
    return jax.shard_map(shards, mesh=mesh, in_specs=in_specs, out_specs=out_specs, check_vma=False)
```

profile of v0, /device:TPU:1, one launch (start us, length us, event | category | flops | bytes accessed | tf_op | source)
XLA Modules:
  0.0 287.1 jit_solution(1144001521220974034)
XLA Ops:
  0.6 1.8 pad_maximum_fusion
  2.5 15.5 %collective-permute-start.3 = (bf16[128,1536]{1,0:T(8,128)(2,1)}, bf16[128,1536]{1,0:T(8,128)(2,1)}, u32[]{:S(2)}, u32[]{:S(2)}) collective-permute-start(bf16[128,1536]{1,0:T(8,128)(2,1)} %pad_maximum_fusion), channel_id=1, source_target_pairs={{32,0},{48,16},{64,32},{80,48},{96,64},{112,80},{128,96},{144,112}... | collective-permute-start | bytes 1179656 | tf_op jit(solution)/shard_map/ppermute | solution.py:12
  17.9 2.9 collective-permute-start.2
  20.8 6.6 %collective-permute-start.1 = (bf16[128,1536]{1,0:T(8,128)(2,1)}, bf16[128,1536]{1,0:T(8,128)(2,1)S(1)}, u32[]{:S(2)}, u32[]{:S(2)}) collective-permute-start(bf16[128,1536]{1,0:T(8,128)(2,1)} %pad_maximum_fusion), channel_id=1, source_target_pairs={{496,0},{0,16},{16,32},{32,48},{48,64},{64,80},{80,96},{96,112},{1... | collective-permute-start | bytes 1179656 | tf_op jit(solution)/shard_map/ppermute | solution.py:12
  27.4 1.9 collective-permute-start
  33.4 26.2 %collective-permute-done.3 = bf16[128,1536]{1,0:T(8,128)(2,1)} collective-permute-done((bf16[128,1536]{1,0:T(8,128)(2,1)}, bf16[128,1536]{1,0:T(8,128)(2,1)}, u32[]{:S(2)}, u32[]{:S(2)}) %collective-permute-start.3) | collective-permute-done | bytes 393248 | tf_op jit(solution)/shard_map/ppermute | solution.py:12
  59.6 1.0 fusion.55
  61.0 3.4 %collective-permute-done.2 = bf16[128,1536]{1,0:T(8,128)(2,1)S(1)} collective-permute-done((bf16[128,1536]{1,0:T(8,128)(2,1)}, bf16[128,1536]{1,0:T(8,128)(2,1)S(1)}, u32[]{:S(2)}, u32[]{:S(2)}) %collective-permute-start.2) | collective-permute-done | bytes 393248 | tf_op jit(solution)/shard_map/ppermute | solution.py:12
  65.1 18.6 %collective-permute-done = bf16[128,1536]{1,0:T(8,128)(2,1)} collective-permute-done((bf16[128,1536]{1,0:T(8,128)(2,1)}, bf16[128,1536]{1,0:T(8,128)(2,1)}, u32[]{:S(2)}, u32[]{:S(2)}) %collective-permute-start) | collective-permute-done | bytes 393248 | tf_op jit(solution)/shard_map/ppermute | solution.py:12
  83.7 1.0 fusion.52
  85.1 1.0 fusion.60
  91.7 1.1 convolution_convert_fusion.6
  93.5 1.1 convolution_convert_fusion.4
  95.0 1.1 convolution_convert_fusion.2
  96.4 1.1 convolution_convert_fusion
  97.8 1.1 convolution_convert_fusion.8
  98.9 1.0 convolution_convert_fusion.9
  100.2 1.1 convolution_convert_fusion.1
  101.4 1.1 convolution_convert_fusion.3
  103.3 100.2 %psum.7 = f32[12]{0:T(128)S(1)} all-reduce(f32[12]{0:T(128)S(1)} %get-tuple-element.15), channel_id=1, replica_groups=mesh['view'=32,'seq'=16] {'view','seq'}, use_global_device_ids=true, to_apply=%region_16.17 | all-reduce | flops 12 | bytes 96 | tf_op jit(solution)/shard_map/psum | solution.py:79
  209.0 1.1 pad_maximum_fusion.1
  210.9 1.8 pad_maximum_fusion.5
  213.6 1.8 pad_maximum_fusion.4
  215.4 1.0 convolution_convert_fusion.7
  216.4 1.1 copy.113
  219.3 2.6 collective-permute-start.5
  221.8 4.8 %collective-permute-start.4 = (bf16[128,1536]{1,0:T(8,128)(2,1)}, bf16[128,1536]{1,0:T(8,128)(2,1)}, u32[]{:S(2)}, u32[]{:S(2)}) collective-permute-start(bf16[128,1536]{1,0:T(8,128)(2,1)} %pad_maximum_fusion.2), channel_id=1, source_target_pairs={{32,0},{48,16},{64,32},{80,48},{96,64},{112,80},{128,96},{144,112}... | collective-permute-start | bytes 1179656 | tf_op jit(solution)/shard_map/ppermute | solution.py:12
  226.7 7.2 %collective-permute-start.6 = (bf16[128,1536]{1,0:T(8,128)(2,1)}, bf16[128,1536]{1,0:T(8,128)(2,1)}, u32[]{:S(2)}, u32[]{:S(2)}) collective-permute-start(bf16[128,1536]{1,0:T(8,128)(2,1)} %pad_maximum_fusion.4), channel_id=1, source_target_pairs={{496,0},{0,16},{16,32},{32,48},{48,64},{64,80},{80,96},{96,112},{1... | collective-permute-start | bytes 1179656 | tf_op jit(solution)/shard_map/ppermute | solution.py:12
  233.8 4.4 %collective-permute-start.7 = (bf16[128,1536]{1,0:T(8,128)(2,1)}, bf16[128,1536]{1,0:T(8,128)(2,1)}, u32[]{:S(2)}, u32[]{:S(2)}) collective-permute-start(bf16[128,1536]{1,0:T(8,128)(2,1)} %pad_maximum_fusion.5), channel_id=1, source_target_pairs={{480,0},{496,16},{0,32},{16,48},{32,64},{48,80},{64,96},{80,112},{... | collective-permute-start | bytes 1179656 | tf_op jit(solution)/shard_map/ppermute | solution.py:12
  240.6 33.6 %collective-permute-done.5 = bf16[128,1536]{1,0:T(8,128)(2,1)S(1)} collective-permute-done((bf16[128,1536]{1,0:T(8,128)(2,1)}, bf16[128,1536]{1,0:T(8,128)(2,1)S(1)}, u32[]{:S(2)}, u32[]{:S(2)}) %collective-permute-start.5) | collective-permute-done | bytes 393248 | tf_op jit(solution)/shard_map/ppermute | solution.py:12
  274.8 10.0 %collective-permute-done.7 = bf16[128,1536]{1,0:T(8,128)(2,1)} collective-permute-done((bf16[128,1536]{1,0:T(8,128)(2,1)}, bf16[128,1536]{1,0:T(8,128)(2,1)}, u32[]{:S(2)}, u32[]{:S(2)}) %collective-permute-start.7) | collective-permute-done | bytes 393248 | tf_op jit(solution)/shard_map/ppermute | solution.py:12
  284.8 1.5 add_convert_fusion
  (88 shorter events, 25.8 us)
Async XLA Ops:
  0.6 28.8 %copy-start.5 = (bf16[1,128,768]{2,1,0:T(8,128)(2,1)S(1)}, bf16[1,128,768]{2,1,0:T(8,128)(2,1)}, u32[]{:S(2)}) copy-start(bf16[1,128,768]{2,1,0:T(8,128)(2,1)} %param.8) | copy-start | bytes 589828
  2.5 57.2 %collective-permute-start.3 = (bf16[128,1536]{1,0:T(8,128)(2,1)}, bf16[128,1536]{1,0:T(8,128)(2,1)}, u32[]{:S(2)}, u32[]{:S(2)}) collective-permute-start(bf16[128,1536]{1,0:T(8,128)(2,1)} %pad_maximum_fusion), channel_id=1, source_target_pairs={{32,0},{48,16},{64,32},{80,48},{96,64},{112,80},{128,96},{144,112}... | collective-permute-start | bytes 1179656 | tf_op jit(solution)/shard_map/ppermute | solution.py:12
  17.9 46.5 %collective-permute-start.2 = (bf16[128,1536]{1,0:T(8,128)(2,1)}, bf16[128,1536]{1,0:T(8,128)(2,1)S(1)}, u32[]{:S(2)}, u32[]{:S(2)}) collective-permute-start(bf16[128,1536]{1,0:T(8,128)(2,1)} %pad_maximum_fusion), channel_id=1, source_target_pairs={{16,0},{32,16},{48,32},{64,48},{80,64},{96,80},{112,96},{128,112},... | collective-permute-start | bytes 1179656 | tf_op jit(solution)/shard_map/ppermute | solution.py:12
  20.8 43.9 %collective-permute-start.1 = (bf16[128,1536]{1,0:T(8,128)(2,1)}, bf16[128,1536]{1,0:T(8,128)(2,1)S(1)}, u32[]{:S(2)}, u32[]{:S(2)}) collective-permute-start(bf16[128,1536]{1,0:T(8,128)(2,1)} %pad_maximum_fusion), channel_id=1, source_target_pairs={{496,0},{0,16},{16,32},{32,48},{48,64},{64,80},{80,96},{96,112},{1... | collective-permute-start | bytes 1179656 | tf_op jit(solution)/shard_map/ppermute | solution.py:12
  27.4 56.3 %collective-permute-start = (bf16[128,1536]{1,0:T(8,128)(2,1)}, bf16[128,1536]{1,0:T(8,128)(2,1)}, u32[]{:S(2)}, u32[]{:S(2)}) collective-permute-start(bf16[128,1536]{1,0:T(8,128)(2,1)} %pad_maximum_fusion), channel_id=1, source_target_pairs={{480,0},{496,16},{0,32},{16,48},{32,64},{48,80},{64,96},{80,112},{... | collective-permute-start | bytes 1179656 | tf_op jit(solution)/shard_map/ppermute | solution.py:12
  29.4 0.9 copy-start.11
  30.5 1.7 copy-start.6
  30.9 0.7 copy-start.14
  32.2 0.9 copy-start.12
  90.7 0.7 copy-start.13
  103.1 100.4 %copy-start = (bf16[12,64,128]{2,1,0:T(8,128)(2,1)S(1)}, bf16[12,64,128]{2,1,0:T(8,128)(2,1)}, u32[]{:S(2)}) copy-start(bf16[12,64,128]{2,1,0:T(8,128)(2,1)} %convolution_convert_fusion.6) | copy-start | bytes 589828
  203.5 0.9 copy-start.1
  204.5 0.9 copy-start.2
  205.4 0.9 copy-start.3
  206.3 0.9 copy-start.4
  207.2 0.9 copy-start.10
  209.0 1.1 copy-start.8
  210.9 1.8 copy-start.7
  216.4 1.1 copy-start.9
  219.3 55.0 %collective-permute-start.5 = (bf16[128,1536]{1,0:T(8,128)(2,1)}, bf16[128,1536]{1,0:T(8,128)(2,1)S(1)}, u32[]{:S(2)}, u32[]{:S(2)}) collective-permute-start(bf16[128,1536]{1,0:T(8,128)(2,1)} %pad_maximum_fusion.3), channel_id=1, source_target_pairs={{16,0},{32,16},{48,32},{64,48},{80,64},{96,80},{112,96},{128,112},... | collective-permute-start | bytes 1179656 | tf_op jit(solution)/shard_map/ppermute | solution.py:12
  221.8 52.9 %collective-permute-start.4 = (bf16[128,1536]{1,0:T(8,128)(2,1)}, bf16[128,1536]{1,0:T(8,128)(2,1)}, u32[]{:S(2)}, u32[]{:S(2)}) collective-permute-start(bf16[128,1536]{1,0:T(8,128)(2,1)} %pad_maximum_fusion.2), channel_id=1, source_target_pairs={{32,0},{48,16},{64,32},{80,48},{96,64},{112,80},{128,96},{144,112}... | collective-permute-start | bytes 1179656 | tf_op jit(solution)/shard_map/ppermute | solution.py:12
  226.7 48.1 %collective-permute-start.6 = (bf16[128,1536]{1,0:T(8,128)(2,1)}, bf16[128,1536]{1,0:T(8,128)(2,1)}, u32[]{:S(2)}, u32[]{:S(2)}) collective-permute-start(bf16[128,1536]{1,0:T(8,128)(2,1)} %pad_maximum_fusion.4), channel_id=1, source_target_pairs={{496,0},{0,16},{16,32},{32,48},{48,64},{64,80},{80,96},{96,112},{1... | collective-permute-start | bytes 1179656 | tf_op jit(solution)/shard_map/ppermute | solution.py:12
  233.8 51.0 %collective-permute-start.7 = (bf16[128,1536]{1,0:T(8,128)(2,1)}, bf16[128,1536]{1,0:T(8,128)(2,1)}, u32[]{:S(2)}, u32[]{:S(2)}) collective-permute-start(bf16[128,1536]{1,0:T(8,128)(2,1)} %pad_maximum_fusion.5), channel_id=1, source_target_pairs={{480,0},{496,16},{0,32},{16,48},{32,64},{48,80},{64,96},{80,112},{... | collective-permute-start | bytes 1179656 | tf_op jit(solution)/shard_map/ppermute | solution.py:12
where the time goes:
time: 290 us; the launch traced here: 287 us
  blocking collectives  100 us (34%)
  waiting for transfers between devices  92.4 us (32%)
  starting transfers between devices  45.8 us (16%)
  matrix products  18.5 us (6%)
  local copies, waits for them, and re-layouts  17 us (6%)
  other arithmetic  11.5 us (4%)
    psum x1, blocking collectives, shards(): gate_sum = lax.psum(gate_part, ('view', 'seq'))  100 us
    ppermute x8, waiting for transfers between devices, from_behind(): return lax.ppermute(block, axis, route)  92.4 us
    ppermute x8, starting transfers between devices, from_behind(): return lax.ppermute(block, axis, route)  45.8 us
    concatenate x5, other arithmetic, shards(): jnp.concatenate([key_term.reshape(tokens, model_width), value_term.reshap...  6.27 us
  transfers between devices with their start and end apart: 8, of which 6 were waited for; matrix products, arithmetic and copies ran while one was open for 2% of the time, Pallas kernels for 0%

commit v1 on v0

v1 whole, which is shorter than its diff:
```python
import functools
import math

import jax
import jax.numpy as jnp
from jax import lax
from jax.experimental import pallas as pl
from jax.experimental.pallas import tpu as pltpu
from jax.sharding import PartitionSpec as P

MESH = pl.DeviceIdType.MESH
LANES = 128
OFFSETS = (0, -2, -1, 1, 2)
FROM_LOW2, FROM_LOW1, FROM_HIGH1, FROM_HIGH2 = 1, 2, 3, 4


def sum_rounds(n_view, n_seq):
    rounds = []
    low = math.gcd(n_view, 8)
    rounds.append(("view", 1, low))
    rounds.append(("view", low, n_view // low))
    low = math.gcd(n_seq, 4)
    rounds.append(("seq", 1, low))
    rounds.append(("seq", low, n_seq // low))
    return [r for r in rounds if r[2] > 1]


def kernel(
    sizes,
    gate_s, neigh_s, counts_s, q_hbm, k_hbm, v_hbm, c_hbm,
    out_ref, dq_ref, dk_ref, dv_ref, gg_ref,
    kv, qg, cot, stats, gacc, gbuf,
    load_sem, kv_send, kv_recv, qg_send, qg_recv, st_send, st_recv, g_send, g_recv,
):
    n_view, n_seq, pairs, head_size = sizes
    tokens = kv.shape[3]
    scale = 1.0 / math.sqrt(head_size)
    me = lax.axis_index("view")
    me_seq = lax.axis_index("seq")
    core = lax.rem(me, 2)
    sibling = me + 1 - 2 * core
    rounds = sum_rounds(n_view, n_seq)

    def view_at(offset):
        return lax.rem(me + offset + n_view, n_view)

    def partner(round_index, step):
        axis, stride, size = rounds[round_index]
        index = me if axis == "view" else me_seq
        digit = lax.rem(index // stride, size)
        other = lax.rem(digit + step, size)
        return {axis: index + (other - digit) * stride}, digit, other

    def load(hbm, column, p, dst):
        return pltpu.make_async_copy(
            hbm.at[0, :, pl.ds(p * LANES, LANES)], dst, load_sem.at[p, column]
        )

    loads = []
    for p in range(pairs):
        loads.append(
            [
                load(k_hbm, 0, p, kv.at[p, 0, 0]),
                load(v_hbm, 1, p, kv.at[p, 0, 1]),
                load(q_hbm, 2, p, qg.at[p, 0, 0]),
                load(c_hbm, 3, p, cot.at[p]),
            ]
        )
    for column in range(4):
        for p in range(pairs):
            loads[p][column].start()

    barrier = pltpu.get_barrier_semaphore()
    greeted = 0
    for offset in OFFSETS[1:]:
        pl.semaphore_signal(
            barrier, inc=1, device_id={"view": view_at(offset)}, device_id_type=MESH
        )
        greeted += 1
    for r in range(len(rounds)):
        for step in range(1, rounds[r][2]):
            pl.semaphore_signal(
                barrier, inc=1, device_id=partner(r, step)[0], device_id_type=MESH
            )
            greeted += 1
    pl.semaphore_wait(barrier, greeted)

    def block_copy(buf, send, recv, p, index):
        src_slot, dst_slot, target = (
            (0, FROM_LOW2, view_at(2)),
            (0, FROM_HIGH2, view_at(-2)),
            (0, 2 + core, sibling),
            (4 - 3 * core, 3 - core, sibling),
        )[index]
        return pltpu.make_async_remote_copy(
            src_ref=buf.at[p, src_slot],
            dst_ref=buf.at[p, dst_slot],
            send_sem=send.at[p, index],
            recv_sem=recv.at[p, dst_slot],
            device_id={"view": target},
            device_id_type=MESH,
        )

    def arrived(buf, send, recv, p, slot):
        pltpu.make_async_remote_copy(
            src_ref=buf.at[p, 0],
            dst_ref=buf.at[p, slot],
            send_sem=send.at[p, 0],
            recv_sem=recv.at[p, slot],
            device_id={"view": sibling},
            device_id_type=MESH,
        ).wait_recv()

    def stat_copy(p, slot):
        return pltpu.make_async_remote_copy(
            src_ref=stats.at[p, 0],
            dst_ref=stats.at[p, 5 - slot],
            send_sem=st_send.at[p, slot],
            recv_sem=st_recv.at[p, 5 - slot],
            device_id={"view": view_at(OFFSETS[slot])},
            device_id_type=MESH,
        )

    for p in range(pairs):
        loads[p][0].wait()
        loads[p][1].wait()
        for index in range(3):
            block_copy(kv, kv_send, kv_recv, p, index).start()
    for p in range(pairs):
        loads[p][2].wait()
        loads[p][3].wait()

    bias = [jnp.float32(0.0)]
    for offset in OFFSETS[1:]:
        view = view_at(offset)
        present = (neigh_s[0, 0] == view) & (counts_s[0] > 0)
        for j in range(1, 4):
            present = present | ((neigh_s[0, j] == view) & (counts_s[0] > j))
        bias.append(jnp.where(present, jnp.float32(0.0), jnp.float32(-jnp.inf)))
    bias_row = jnp.concatenate([jnp.full((1, tokens), b, jnp.float32) for b in bias], axis=1)
    lane = lax.broadcasted_iota(jnp.int32, (tokens, LANES), 1)
    low_half = lane < head_size

    def stacked(block):
        zero = jnp.zeros_like(block)
        return jnp.concatenate(
            [jnp.where(low_half, block, zero), jnp.where(low_half, zero, block)], axis=0
        )

    def unstacked(block):
        return jnp.where(low_half, block[:tokens], block[tokens:])

    def dot_t(a, b):
        return lax.dot_general(
            a, b, (((1,), (1,)), ((), ())), preferred_element_type=jnp.float32
        )

    def dot(a, b):
        return jnp.dot(a, b, preferred_element_type=jnp.float32)

    gacc[...] = jnp.zeros_like(gacc)

    def query_side(p):
        columns = pl.ds(pl.multiple_of(p * LANES, LANES), LANES)
        gate_row = jnp.where(low_half[:1], gate_s[2 * p], gate_s[2 * p + 1])
        cot_block = cot[p].astype(jnp.float32)
        grad = (gate_row * cot_block).astype(jnp.bfloat16)
        qg[p, 0, 1] = grad
        keys = kv[p, :, 0].reshape(5 * tokens, LANES)
        values = kv[p, :, 1].reshape(5 * tokens, LANES)
        scores = dot_t(stacked(qg[p, 0, 0]), keys) * scale + bias_row
        top = jnp.max(scores, axis=1, keepdims=True)
        raised = jnp.exp(scores - top)
        total = jnp.sum(raised, axis=1, keepdims=True)
        probs = raised * (1.0 / total)
        log_total = top + jnp.log(total)
        attended = unstacked(dot(probs.astype(jnp.bfloat16), values))
        out_ref[0, :, columns] = (gate_row * attended).astype(jnp.bfloat16)
        gacc[pl.ds(p, 1), :] = jnp.sum(cot_block * attended, axis=0, keepdims=True)
        product = grad.astype(jnp.float32) * attended
        delta_low = jnp.sum(jnp.where(low_half, product, 0.0), axis=1, keepdims=True)
        delta_high = jnp.sum(jnp.where(low_half, 0.0, product), axis=1, keepdims=True)
        table = jnp.where(lane == 0, log_total[:tokens], log_total[tokens:])
        table = jnp.where(lane == 2, delta_low, table)
        table = jnp.where(lane == 3, delta_high, table)
        stats[p, 0] = jnp.transpose(table)[:8]
        for slot in range(1, 5):
            stat_copy(p, slot).start()
        for index in range(3):
            block_copy(qg, qg_send, qg_recv, p, index).start()
        prob_grad = dot_t(stacked(grad), values)
        delta = jnp.concatenate([delta_low, delta_high], axis=0)
        score_grad = (probs * (prob_grad - delta) * scale).astype(jnp.bfloat16)
        dq_ref[0, :, columns] = unstacked(dot(score_grad, keys)).astype(jnp.bfloat16)

    def key_side(p):
        columns = pl.ds(pl.multiple_of(p * LANES, LANES), LANES)
        queries = qg[p, :, 0].reshape(5 * tokens, LANES)
        grads = qg[p, :, 1].reshape(5 * tokens, LANES)
        tables = [stats[p, slot] for slot in range(5)]
        rows = jnp.concatenate(tables, axis=1)

        def both(first, second):
            shape = (tokens, 5 * tokens)
            return jnp.concatenate(
                [jnp.broadcast_to(first, shape), jnp.broadcast_to(second, shape)], axis=0
            )

        log_total = both(rows[0:1] - bias_row, rows[1:2] - bias_row)
        delta = both(rows[2:3], rows[3:4])
        scores = dot_t(stacked(kv[p, 0, 0]), queries) * scale
        probs = jnp.exp(scores - log_total)
        dv_ref[0, :, columns] = unstacked(dot(probs.astype(jnp.bfloat16), grads)).astype(
            jnp.bfloat16
        )
        prob_grad = dot_t(stacked(kv[p, 0, 1]), grads)
        score_grad = (probs * (prob_grad - delta) * scale).astype(jnp.bfloat16)
        dk_ref[0, :, columns] = unstacked(dot(score_grad, queries)).astype(jnp.bfloat16)

    def gate_copy(r, step):
        target, digit, other = partner(r, step)
        return pltpu.make_async_remote_copy(
            src_ref=gbuf.at[r, digit],
            dst_ref=gbuf.at[r, digit],
            send_sem=g_send.at[r, step],
            recv_sem=g_recv.at[r, digit],
            device_id=target,
            device_id_type=MESH,
        )

    def gate_arrived(r, step):
        target, digit, other = partner(r, step)
        pltpu.make_async_remote_copy(
            src_ref=gbuf.at[r, digit],
            dst_ref=gbuf.at[r, other],
            send_sem=g_send.at[r, step],
            recv_sem=g_recv.at[r, other],
            device_id=target,
            device_id_type=MESH,
        ).wait_recv()

    def gate_total(r):
        for step in range(1, rounds[r][2]):
            gate_arrived(r, step)
        total = gbuf[r, 0]
        for i in range(1, rounds[r][2]):
            total = total + gbuf[r, i]
        return total

    def gate_send(r):
        block = gacc[...] if r == 0 else gate_total(r - 1)
        gbuf[r, partner(r, 0)[1]] = block
        for step in range(1, rounds[r][2]):
            gate_copy(r, step).start()

    def first_step(i, carry):
        @pl.when(i < pairs)
        def _():
            arrived(kv, kv_send, kv_recv, i, FROM_LOW2)
            arrived(kv, kv_send, kv_recv, i, FROM_HIGH2)
            block_copy(kv, kv_send, kv_recv, i, 3).start()

        @pl.when(i > 0)
        def _():
            arrived(kv, kv_send, kv_recv, i - 1, FROM_LOW1)
            arrived(kv, kv_send, kv_recv, i - 1, FROM_HIGH1)
            query_side(i - 1)

        return carry

    lax.fori_loop(0, pairs + 1, first_step, 0)

    def second_step(i, carry):
        for r in range(len(rounds)):

            @pl.when(i == r)
            def _():
                gate_send(r)

        @pl.when(i < pairs)
        def _():
            arrived(qg, qg_send, qg_recv, i, FROM_LOW2)
            arrived(qg, qg_send, qg_recv, i, FROM_HIGH2)
            block_copy(qg, qg_send, qg_recv, i, 3).start()

        @pl.when(i > 0)
        def _():
            for slot in (FROM_LOW1, FROM_HIGH1):
                arrived(qg, qg_send, qg_recv, i - 1, slot)
            for slot in range(1, 5):
                stat_copy(i - 1, slot).wait_recv()
            key_side(i - 1)

        return carry

    lax.fori_loop(0, pairs + 1, second_step, 0)

    total = gate_total(len(rounds) - 1)
    low_row = lax.broadcasted_iota(jnp.int32, total.shape, 1) < head_size
    sums_low = jnp.sum(jnp.where(low_row, total, 0.0), axis=1, keepdims=True)
    sums_high = jnp.sum(jnp.where(low_row, 0.0, total), axis=1, keepdims=True)
    place = lax.broadcasted_iota(jnp.int32, total.shape, 1)
    row = lax.broadcasted_iota(jnp.int32, total.shape, 0)
    spread = jnp.where(place == 2 * row, sums_low, 0.0) + jnp.where(
        place == 2 * row + 1, sums_high, 0.0
    )
    divisor = math.sqrt(n_view * n_seq * tokens * head_size)
    gg_ref[...] = jnp.sum(spread, axis=0, keepdims=True) * (1.0 / divisor)

    def drain(p, carry):
        for index in range(4):
            block_copy(kv, kv_send, kv_recv, p, index).wait_send()
            block_copy(qg, qg_send, qg_recv, p, index).wait_send()
        for slot in range(1, 5):
            stat_copy(p, slot).wait_send()
        return carry

    lax.fori_loop(0, pairs, drain, 0)
    for r in range(len(rounds)):
        for step in range(1, rounds[r][2]):
            gate_copy(r, step).wait_send()


def shards(query_rows, key_rows, value_rows, head_gate, cotangent, neighbours, counts):
    _, tokens, width = query_rows.shape
    heads = head_gate.shape[0]
    pairs = width // LANES
    n_view, n_seq = lax.axis_size("view"), lax.axis_size("seq")
    rounds = sum_rounds(n_view, n_seq)
    most = max(r[2] for r in rounds)
    smem = pl.BlockSpec(memory_space=pltpu.SMEM)
    vmem = pl.BlockSpec(memory_space=pltpu.VMEM)
    anywhere = pl.BlockSpec(memory_space=pl.ANY)
    rows = jax.ShapeDtypeStruct(query_rows.shape, jnp.bfloat16)
    dma = pltpu.SemaphoreType.DMA
    out, dq, dk, dv, gate = pl.pallas_call(
        functools.partial(kernel, (n_view, n_seq, pairs, width // heads)),
        out_shape=[rows] * 4 + [jax.ShapeDtypeStruct((1, LANES), jnp.float32)],
        in_specs=[smem] * 3 + [anywhere] * 4,
        out_specs=[vmem] * 5,
        scratch_shapes=[
            pltpu.VMEM((pairs, 5, 2, tokens, LANES), jnp.bfloat16),
            pltpu.VMEM((pairs, 5, 2, tokens, LANES), jnp.bfloat16),
            pltpu.VMEM((pairs, tokens, LANES), jnp.bfloat16),
            pltpu.VMEM((pairs, 5, 8, LANES), jnp.float32),
            pltpu.VMEM((8, LANES), jnp.float32),
            pltpu.VMEM((len(rounds), most, 8, LANES), jnp.float32),
            dma((pairs, 4)),
            dma((pairs, 4)),
            dma((pairs, 5)),
            dma((pairs, 4)),
            dma((pairs, 5)),
            dma((pairs, 5)),
            dma((pairs, 5)),
            dma((len(rounds), most)),
            dma((len(rounds), most)),
        ],
        compiler_params=pltpu.CompilerParams(
            collective_id=0, has_side_effects=True, vmem_limit_bytes=40 * 1024 * 1024
        ),
        cost_estimate=pl.CostEstimate(
            flops=2 * 8 * 5 * heads * tokens * tokens * 64, bytes_accessed=3200000, transcendentals=0
        ),
    )(head_gate, neighbours, counts, query_rows, key_rows, value_rows, cotangent)
    return out, dq, dk, dv, gate[0, :heads]


def solution(mesh):
    in_specs = (
        P("view", "seq", None),
        P("view", "seq", None),
        P("view", "seq", None),
        P(),
        P("view", "seq", None),
        P("view", None),
        P("view"),
    )
    out_specs = (
        P("view", "seq", None),
        P("view", "seq", None),
        P("view", "seq", None),
        P("view", "seq", None),
        P(),
    )
    return jax.shard_map(shards, mesh=mesh, in_specs=in_specs, out_specs=out_specs, check_vma=False)
```

time: 290 us -> 116 us (0.40)
  Pallas kernels: 0 us -> 108 us
  blocking collectives: 100 us -> 0 us
  waiting for transfers between devices: 92.4 us -> 0 us
  starting transfers between devices: 45.8 us -> 0 us
  matrix products: 18.5 us -> 0 us
  other arithmetic: 11.5 us -> 0 us
  local copies, waits for them, and re-layouts: 17 us -> 6.93 us
    pallas_call x0 -> x1, Pallas kernels: none -> 108 us  [shards(): pl.pallas_call(functools.partial(kernel, (n_view, n_seq, pairs, width //...]
    psum x1 -> x0, blocking collectives: 100 us -> none  [shards(): gate_sum = lax.psum(gate_part, ('view', 'seq'))]
    ppermute x8 -> x0, waiting for transfers between devices: 92.4 us -> none  [from_behind(): return lax.ppermute(block, axis, route)]
    ppermute x8 -> x0, starting transfers between devices: 45.8 us -> none  [from_behind(): return lax.ppermute(block, axis, route)]
    dot_general x30 -> x0, matrix products: 18.5 us -> none  [the longest x5 5.34 us: shards(): jnp.einsum('hbc,bhd->chd', block_probs_low, attn_grad, preferred_element_...]
    concatenate x6 -> x0, other arithmetic: 8.1 us -> none  [the longest x5 6.27 us: shards(): jnp.concatenate([key_term.reshape(tokens, model_width), value_term.reshap...]
    reshape x11 -> x0, local copies, waits for them, and re-layouts: 7.92 us -> none  [the longest x5 3.71 us: shards(): key_term.reshape(tokens, model_width)]
    slice x12 -> x0, local copies, waits for them, and re-layouts: 3.45 us -> none  [the longest x7 1.75 us: shards(): entry[:, model_width:].reshape(tokens, head_count, head_size)]
  transfers between devices with their start and end apart: 8 -> 0, of which waited for: 6 -> 0; matrix products, arithmetic and copies ran while one was open for 2% -> 0% of each run, Pallas kernels for 0% -> 0%
where the time goes in v1:
time: 116 us
  Pallas kernels  108 us (93%)
  local copies, waits for them, and re-layouts  6.93 us (6%)
  between operations  1.35 us (1%)
    pallas_call x1, Pallas kernels, shards(): pl.pallas_call(functools.partial(kernel, (n_view, n_seq, pairs, width //...  108 us
    unnamed x16, local copies, waits for them, and re-layouts  6.41 us

profile of v1, /device:TPU:1, one launch (start us, length us, event | category | flops | bytes accessed | tf_op | source)
XLA Modules:
  0.0 115.9 jit_solution(6507523112395654021)
XLA Ops:
  0.6 0.0 copy-start.5
  0.6 0.0 copy-start.4
  1.3 0.0 copy-done.5
  1.3 0.0 copy-done.4
  1.3 0.0 copy-start
  1.3 0.9 copy-done
  2.3 0.0 copy-start.1
  2.3 0.9 copy-done.1
  3.2 0.0 copy-start.2
  3.2 0.9 copy-done.2
  4.1 0.0 copy-start.3
  4.1 0.9 copy-done.3
  5.0 107.6 %shard_map.110 = (bf16[1,128,768]{2,1,0:T(8,128)(2,1)S(1)}, bf16[1,128,768]{2,1,0:T(8,128)(2,1)S(1)}, bf16[1,128,768]{2,1,0:T(8,128)(2,1)S(1)}, bf16[1,128,768]{2,1,0:T(8,128)(2,1)S(1)}, f32[1,128]{1,0:T(1,128)S(1)}) custom-call(f32[12]{0:T(128)S(1)} %copy-done.4, s32[1,4]{1,0:T(1,128)S(1)} %copy-done.5, s32[1]{0:T(128)S(6)} %copy.16.counts_s, ...), custom_call_target="tpu_custom_call" | custom-call | flops 1006632960 | bytes 3200000 | tf_op jit(solution)/shard_map/pallas_call | solution.py:336
  112.7 0.5 slice_bitcast_fusion
  113.2 0.7 copy.17
  113.9 0.7 copy.18
  114.6 0.7 copy.19
  115.2 0.7 copy.20
Async XLA Ops:
  0.6 0.7 copy-start.5
  0.6 0.7 copy-start.4
  1.3 0.9 copy-start
  2.3 0.9 copy-start.1
  3.2 0.9 copy-start.2
  4.1 0.9 copy-start.3

commit v2 on v1

v2 whole, which is shorter than its diff:
```python
import functools
import math

import jax
import jax.numpy as jnp
from jax import lax
from jax.experimental import pallas as pl
from jax.experimental.pallas import tpu as pltpu
from jax.sharding import PartitionSpec as P

MESH = pl.DeviceIdType.MESH
LANES = 128
OFFSETS = (0, -2, -1, 1, 2)
FROM_LOW2, FROM_LOW1, FROM_HIGH1, FROM_HIGH2 = 1, 2, 3, 4
KEYS, QUERIES, STATS = 0, 1, 2


def sum_rounds(n_view, n_seq):
    high = math.gcd(n_view // 2, 4)
    low = math.gcd(n_seq, 4)
    groups = [
        [("view", 1, 2)],
        [("view", 2 * high, n_view // (2 * high))],
        [("seq", low, n_seq // low)],
        [("view", 2, high), ("seq", 1, low)],
    ]
    return [g for g in groups if group_size(g) > 1]


def group_size(group):
    return math.prod(size for _, _, size in group)


def kernel(
    sizes,
    counts_s, gate_hbm, neigh_hbm, q_hbm, k_hbm, v_hbm, c_hbm,
    out_ref, dq_ref, dk_ref, dv_ref, gg_ref,
    gate_s, neigh_s, kv, qg, cot, stats, gacc, gbuf,
    small_sem, load_sem, send_sem, recv_sem, g_send, g_recv,
):
    n_view, n_seq, pairs, head_size = sizes
    tokens = kv.shape[3]
    scale = 1.0 / math.sqrt(head_size)
    me = lax.axis_index("view")
    me_seq = lax.axis_index("seq")
    core = lax.rem(me, 2)
    sibling = me + 1 - 2 * core
    rounds = sum_rounds(n_view, n_seq)

    def view_at(offset):
        return lax.rem(me + offset + n_view, n_view)

    def partner(group, step):
        index = {"view": me, "seq": me_seq}
        place = 0
        for axis, stride, size in group:
            place = place * size + lax.rem(index[axis] // stride, size)
        other = lax.rem(place + step, group_size(group))
        target = {}
        rest = other
        for axis, stride, size in reversed(group):
            digit = lax.rem(index[axis] // stride, size)
            target[axis] = index[axis] + (lax.rem(rest, size) - digit) * stride
            rest = rest // size
        return target, place, other

    def load(hbm, column, p, dst):
        return pltpu.make_async_copy(
            hbm.at[0, :, pl.ds(p * LANES, LANES)], dst, load_sem.at[p, column]
        )

    loads = []
    for p in range(pairs):
        loads.append(
            [
                load(k_hbm, 0, p, kv.at[p, 0, 0]),
                load(v_hbm, 1, p, kv.at[p, 0, 1]),
                load(q_hbm, 2, p, qg.at[p, 0, 0]),
                load(c_hbm, 3, p, cot.at[p]),
            ]
        )
    for column in range(4):
        for p in range(pairs):
            loads[p][column].start()

    smalls = [
        pltpu.make_async_copy(src, dst, small_sem.at[i])
        for i, (src, dst) in enumerate(((gate_hbm, gate_s), (neigh_hbm, neigh_s)))
    ]
    for copy in smalls:
        copy.start()

    barrier = pltpu.get_barrier_semaphore()
    greeted = 0
    for offset in OFFSETS[1:]:
        pl.semaphore_signal(
            barrier, inc=1, device_id={"view": view_at(offset)}, device_id_type=MESH
        )
        greeted += 1
    for group in rounds:
        for step in range(1, group_size(group)):
            pl.semaphore_signal(
                barrier, inc=1, device_id=partner(group, step)[0], device_id_type=MESH
            )
            greeted += 1
    pl.semaphore_wait(barrier, greeted)

    def views(kind, p, slot):
        if kind is STATS:
            return stats.at[p, slot, pl.ds(0, 4)]
        return (kv if kind is KEYS else qg).at[p, slot]

    def block_copy(kind, p, index):
        src_slot, dst_slot, target = (
            (0, FROM_LOW2, view_at(2)),
            (0, FROM_HIGH2, view_at(-2)),
            (0, 2 + core, sibling),
            (4 - 3 * core, 3 - core, sibling),
        )[index]
        return pltpu.make_async_remote_copy(
            src_ref=views(kind, p, src_slot),
            dst_ref=views(kind, p, dst_slot),
            send_sem=send_sem.at[kind, p, index],
            recv_sem=recv_sem.at[kind, p, dst_slot],
            device_id={"view": target},
            device_id_type=MESH,
        )

    def send(kind, p):
        for index in range(3):
            block_copy(kind, p, index).start()

    def arrived(kind, p, slot):
        pltpu.make_async_remote_copy(
            src_ref=views(kind, p, 0),
            dst_ref=views(kind, p, slot),
            send_sem=send_sem.at[kind, p, 0],
            recv_sem=recv_sem.at[kind, p, slot],
            device_id={"view": sibling},
            device_id_type=MESH,
        ).wait_recv()

    def pass_on(kind, p):
        arrived(kind, p, FROM_LOW2)
        arrived(kind, p, FROM_HIGH2)
        block_copy(kind, p, 3).start()

    def chip_arrived(kind, p):
        arrived(kind, p, FROM_LOW1)
        arrived(kind, p, FROM_HIGH1)

    def sent(kind, p):
        for index in range(4):
            block_copy(kind, p, index).wait_send()

    for p in range(pairs):
        loads[p][0].wait()
        loads[p][1].wait()
        send(KEYS, p)
    for p in range(pairs):
        loads[p][2].wait()
        loads[p][3].wait()
    for copy in smalls:
        copy.wait()

    bias = [jnp.float32(0.0)]
    for offset in OFFSETS[1:]:
        view = view_at(offset)
        present = (neigh_s[0, 0] == view) & (counts_s[0] > 0)
        for j in range(1, 4):
            present = present | ((neigh_s[0, j] == view) & (counts_s[0] > j))
        bias.append(jnp.where(present, jnp.float32(0.0), jnp.float32(-jnp.inf)))
    bias_row = jnp.concatenate([jnp.full((1, tokens), b, jnp.float32) for b in bias], axis=1)
    lane = lax.broadcasted_iota(jnp.int32, (tokens, LANES), 1)
    low_half = lane < head_size

    def stacked(block):
        zero = jnp.zeros_like(block)
        return jnp.concatenate(
            [jnp.where(low_half, block, zero), jnp.where(low_half, zero, block)], axis=0
        )

    def unstacked(block):
        return jnp.where(low_half, block[:tokens], block[tokens:])

    def dot_t(a, b):
        return lax.dot_general(
            a, b, (((1,), (1,)), ((), ())), preferred_element_type=jnp.float32
        )

    def dot(a, b):
        return jnp.dot(a, b, preferred_element_type=jnp.float32)

    gacc[...] = jnp.zeros_like(gacc)

    def query_side(p):
        columns = pl.ds(pl.multiple_of(p * LANES, LANES), LANES)
        gate_row = jnp.where(low_half[:1], gate_s[2 * p], gate_s[2 * p + 1])
        cot_block = cot[p].astype(jnp.float32)
        grad = (gate_row * cot_block).astype(jnp.bfloat16)
        qg[p, 0, 1] = grad
        keys = kv[p, :, 0].reshape(5 * tokens, LANES)
        values = kv[p, :, 1].reshape(5 * tokens, LANES)
        scores = dot_t(stacked(qg[p, 0, 0]), keys) * scale + bias_row
        top = jnp.max(scores, axis=1, keepdims=True)
        raised = jnp.exp(scores - top)
        total = jnp.sum(raised, axis=1, keepdims=True)
        probs = raised * (1.0 / total)
        log_total = top + jnp.log(total)
        attended = unstacked(dot(probs.astype(jnp.bfloat16), values))
        out_ref[0, :, columns] = (gate_row * attended).astype(jnp.bfloat16)
        gacc[pl.ds(p, 1), :] = jnp.sum(cot_block * attended, axis=0, keepdims=True)
        product = grad.astype(jnp.float32) * attended
        delta_low = jnp.sum(jnp.where(low_half, product, 0.0), axis=1, keepdims=True)
        delta_high = jnp.sum(jnp.where(low_half, 0.0, product), axis=1, keepdims=True)
        table = jnp.where(lane == 0, log_total[:tokens], log_total[tokens:])
        table = jnp.where(lane == 2, delta_low, table)
        table = jnp.where(lane == 3, delta_high, table)
        stats[p, 0] = jnp.transpose(table)[:8]
        send(STATS, p)

        @pl.when(p < pairs - 1)
        def _():
            send(QUERIES, p)

        prob_grad = dot_t(stacked(grad), values)
        delta = jnp.concatenate([delta_low, delta_high], axis=0)
        score_grad = (probs * (prob_grad - delta) * scale).astype(jnp.bfloat16)
        dq_ref[0, :, columns] = unstacked(dot(score_grad, keys)).astype(jnp.bfloat16)

    def key_side(p):
        columns = pl.ds(pl.multiple_of(p * LANES, LANES), LANES)
        queries = qg[p, :, 0].reshape(5 * tokens, LANES)
        grads = qg[p, :, 1].reshape(5 * tokens, LANES)
        tables = [stats[p, slot] for slot in range(5)]
        rows = jnp.concatenate(tables, axis=1)

        def both(first, second):
            shape = (tokens, 5 * tokens)
            return jnp.concatenate(
                [jnp.broadcast_to(first, shape), jnp.broadcast_to(second, shape)], axis=0
            )

        log_total = both(rows[0:1] - bias_row, rows[1:2] - bias_row)
        delta = both(rows[2:3], rows[3:4])
        scores = dot_t(stacked(kv[p, 0, 0]), queries) * scale
        probs = jnp.exp(scores - log_total)
        dv_ref[0, :, columns] = unstacked(dot(probs.astype(jnp.bfloat16), grads)).astype(
            jnp.bfloat16
        )
        prob_grad = dot_t(stacked(kv[p, 0, 1]), grads)
        score_grad = (probs * (prob_grad - delta) * scale).astype(jnp.bfloat16)
        dk_ref[0, :, columns] = unstacked(dot(score_grad, queries)).astype(jnp.bfloat16)

    def gate_copy(r, step):
        target, place, _ = partner(rounds[r], step)
        row = gbuf.at[r, place, pl.ds(0, 1)]
        return pltpu.make_async_remote_copy(
            src_ref=row,
            dst_ref=row,
            send_sem=g_send.at[r, step],
            recv_sem=g_recv.at[r, place],
            device_id=target,
            device_id_type=MESH,
        )

    def gate_send(r, row):
        gbuf[r, partner(rounds[r], 0)[1], pl.ds(0, 1)] = row
        for step in range(1, group_size(rounds[r])):
            gate_copy(r, step).start()

    def gate_total(r):
        for step in range(1, group_size(rounds[r])):
            target, place, other = partner(rounds[r], step)
            pltpu.make_async_remote_copy(
                src_ref=gbuf.at[r, place, pl.ds(0, 1)],
                dst_ref=gbuf.at[r, other, pl.ds(0, 1)],
                send_sem=g_send.at[r, step],
                recv_sem=g_recv.at[r, other],
                device_id=target,
                device_id_type=MESH,
            ).wait_recv()
        total = gbuf[r, 0, pl.ds(0, 1)]
        for i in range(1, group_size(rounds[r])):
            total = total + gbuf[r, i, pl.ds(0, 1)]
        return total

    def first_step(i, carry):
        @pl.when(i < pairs)
        def _():
            pass_on(KEYS, i)

        @pl.when(i > 0)
        def _():
            chip_arrived(KEYS, i - 1)
            query_side(i - 1)

        return carry

    lax.fori_loop(0, pairs + 1, first_step, 0)

    sums = gacc[...]
    place = lax.broadcasted_iota(jnp.int32, sums.shape, 1)
    row = lax.broadcasted_iota(jnp.int32, sums.shape, 0)
    sums_low = jnp.sum(jnp.where(place < head_size, sums, 0.0), axis=1, keepdims=True)
    sums_high = jnp.sum(jnp.where(place < head_size, 0.0, sums), axis=1, keepdims=True)
    spread = jnp.where(place == 2 * row, sums_low, 0.0) + jnp.where(
        place == 2 * row + 1, sums_high, 0.0
    )
    gate_row = jnp.sum(spread, axis=0, keepdims=True)
    for r in range(len(rounds) - 1):
        gate_send(r, gate_row)
        gate_row = gate_total(r)
    gate_send(len(rounds) - 1, gate_row)
    send(QUERIES, pairs - 1)

    def second_step(i, carry):
        pass_on(STATS, i)
        pass_on(QUERIES, i)

        @pl.when(i > 0)
        def _():
            chip_arrived(STATS, i - 1)
            chip_arrived(QUERIES, i - 1)
            key_side(i - 1)
            sent(KEYS, i - 1)
            sent(STATS, i - 1)
            sent(QUERIES, i - 1)

        return carry

    last = pairs - 1
    lax.fori_loop(0, last, second_step, 0)
    chip_arrived(STATS, last - 1)
    chip_arrived(QUERIES, last - 1)
    key_side(last - 1)
    pass_on(STATS, last)
    divisor = math.sqrt(n_view * n_seq * tokens * head_size)
    gg_ref[...] = gate_total(len(rounds) - 1) * (1.0 / divisor)
    for r in range(len(rounds)):
        for step in range(1, group_size(rounds[r])):
            gate_copy(r, step).wait_send()
    sent(KEYS, last - 1)
    sent(STATS, last - 1)
    sent(QUERIES, last - 1)
    sent(KEYS, last)
    chip_arrived(STATS, last)
    sent(STATS, last)
    pass_on(QUERIES, last)
    chip_arrived(QUERIES, last)
    key_side(last)
    sent(QUERIES, last)


def hand_over(out, dq, dk, dv, gate, out_ref, dq_ref, dk_ref, dv_ref, gate_ref, sem):
    pairs = ((out, out_ref), (dq, dq_ref), (dk, dk_ref), (dv, dv_ref))
    copies = [pltpu.make_async_copy(a, b, sem.at[i]) for i, (a, b) in enumerate(pairs)]
    for copy in copies:
        copy.start()
    gate_ref[...] = gate[0, : gate_ref.shape[0]]
    for copy in copies:
        copy.wait()


def shards(query_rows, key_rows, value_rows, head_gate, cotangent, neighbours, counts):
    _, tokens, width = query_rows.shape
    heads = head_gate.shape[0]
    pairs = width // LANES
    n_view, n_seq = lax.axis_size("view"), lax.axis_size("seq")
    rounds = sum_rounds(n_view, n_seq)
    most = max(group_size(g) for g in rounds)
    vmem = pl.BlockSpec(memory_space=pltpu.VMEM)
    hbm = pl.BlockSpec(memory_space=pltpu.HBM)
    rows = jax.ShapeDtypeStruct(query_rows.shape, jnp.bfloat16)
    dma = pltpu.SemaphoreType.DMA
    operands = (head_gate, neighbours, query_rows, key_rows, value_rows, cotangent)
    results = pl.pallas_call(
        functools.partial(kernel, (n_view, n_seq, pairs, width // heads)),
        out_shape=[pltpu.VMEM(query_rows.shape, jnp.bfloat16)] * 4
        + [pltpu.VMEM((1, LANES), jnp.float32)],
        in_specs=[pl.BlockSpec(memory_space=pltpu.SMEM)] + [hbm] * 6,
        out_specs=[vmem] * 5,
        scratch_shapes=[
            pltpu.SMEM(head_gate.shape, jnp.float32),
            pltpu.SMEM(neighbours.shape, jnp.int32),
            pltpu.VMEM((pairs, 5, 2, tokens, LANES), jnp.bfloat16),
            pltpu.VMEM((pairs, 5, 2, tokens, LANES), jnp.bfloat16),
            pltpu.VMEM((pairs, tokens, LANES), jnp.bfloat16),
            pltpu.VMEM((pairs, 5, 8, LANES), jnp.float32),
            pltpu.VMEM((8, LANES), jnp.float32),
            pltpu.VMEM((len(rounds), most, 8, LANES), jnp.float32),
            dma((2,)),
            dma((pairs, 4)),
            dma((3, pairs, 4)),
            dma((3, pairs, 5)),
            dma((len(rounds), most)),
            dma((len(rounds), most)),
        ],
        compiler_params=pltpu.CompilerParams(
            collective_id=0, has_side_effects=True, vmem_limit_bytes=40 * 1024 * 1024
        ),
        cost_estimate=pl.CostEstimate(
            flops=2 * 8 * 5 * heads * tokens * tokens * 64, bytes_accessed=3200000, transcendentals=0
        ),
    )(counts, *(pltpu.with_memory_space_constraint(a, pltpu.HBM) for a in operands))
    return pl.pallas_call(
        hand_over,
        out_shape=[rows] * 4 + [jax.ShapeDtypeStruct((heads,), jnp.float32)],
        in_specs=[vmem] * 5,
        out_specs=[hbm] * 4 + [vmem],
        scratch_shapes=[dma((4,))],
    )(*(pltpu.with_memory_space_constraint(a, pltpu.VMEM) for a in results))


def solution(mesh):
    in_specs = (
        P("view", "seq", None),
        P("view", "seq", None),
        P("view", "seq", None),
        P(),
        P("view", "seq", None),
        P("view", None),
        P("view"),
    )
    out_specs = (
        P("view", "seq", None),
        P("view", "seq", None),
        P("view", "seq", None),
        P("view", "seq", None),
        P(),
    )
    return jax.shard_map(shards, mesh=mesh, in_specs=in_specs, out_specs=out_specs, check_vma=False)
```

time: 116 us -> 96.8 us (0.83)
  Pallas kernels: 108 us -> 95.4 us
  local copies, waits for them, and re-layouts: 6.93 us -> 0 us
    pallas_call x1, Pallas kernels: 108 us -> 94 us  [shards(): pl.pallas_call(functools.partial(kernel, (n_view, n_seq, pairs, width //...]
    unnamed x16 -> x0, local copies, waits for them, and re-layouts: 6.41 us -> none
    pallas_call x0 -> x1, Pallas kernels: none -> 1.42 us  [shards(): pl.pallas_call(hand_over, out_shape=[rows] * 4 + [jax.ShapeDtypeStruct((h...]
where the time goes in v2:
time: 96.8 us; the launch traced here: 96.7 us
  Pallas kernels  95.4 us (99%)
  between operations  1.29 us (1%)
    pallas_call x1, Pallas kernels, shards(): pl.pallas_call(functools.partial(kernel, (n_view, n_seq, pairs, width //...  94 us

profile of v2, /device:TPU:1, one launch (start us, length us, event | category | flops | bytes accessed | tf_op | source)
XLA Modules:
  0.0 96.7 jit_solution(10830619542541311548)
XLA Ops:
  1.3 94.0 %shard_map.110 = (bf16[1,128,768]{2,1,0:T(8,128)(2,1)S(1)}, bf16[1,128,768]{2,1,0:T(8,128)(2,1)S(1)}, bf16[1,128,768]{2,1,0:T(8,128)(2,1)S(1)}, bf16[1,128,768]{2,1,0:T(8,128)(2,1)S(1)}, f32[1,128]{1,0:T(1,128)S(1)}) custom-call(s32[1]{0:T(128)S(6)} %copy.12.counts_s, f32[12]{0:T(128)} %gate_hbm.1, s32[1,4]{1,0:T(1,128)} %neigh_hbm.1, ...), custom_call_target="tpu_custom_call" | custom-call | flops 1006632960 | bytes 3200000 | tf_op jit(solution)/shard_map/pallas_call | solution.py:377
  95.3 1.4 %shard_map.111 = (bf16[1,128,768]{2,1,0:T(8,128)(2,1)}, bf16[1,128,768]{2,1,0:T(8,128)(2,1)}, bf16[1,128,768]{2,1,0:T(8,128)(2,1)}, bf16[1,128,768]{2,1,0:T(8,128)(2,1)}, f32[12]{0:T(128)}) custom-call(bf16[1,128,768]{2,1,0:T(8,128)(2,1)S(1)} %get-tuple-element.10.out, bf16[1,128,768]{2,1,0:T(8,128)(2,1)S(1)} %get-tuple-element.11.dq, ...), custom_call_target="tpu_custom_call" | custom-call | tf_op jit(solution)/shard_map/pallas_call | solution.py:406

commit v3 on v2

--- a/solution.py
+++ b/solution.py
@@ -12,23 +12,18 @@
 LANES = 128
 OFFSETS = (0, -2, -1, 1, 2)
 FROM_LOW2, FROM_LOW1, FROM_HIGH1, FROM_HIGH2 = 1, 2, 3, 4
+WINDOWS = (5, 3, 3, 5)
 KEYS, QUERIES, STATS = 0, 1, 2
 
 
-def sum_rounds(n_view, n_seq):
+Z_STEPS = ((1, 2), (-1, -2), (2, 4))
+
+
+def sum_groups(n_view, n_seq):
     high = math.gcd(n_view // 2, 4)
     low = math.gcd(n_seq, 4)
-    groups = [
-        [("view", 1, 2)],
-        [("view", 2 * high, n_view // (2 * high))],
-        [("seq", low, n_seq // low)],
-        [("view", 2, high), ("seq", 1, low)],
-    ]
-    return [g for g in groups if group_size(g) > 1]
-
-
-def group_size(group):
-    return math.prod(size for _, _, size in group)
+    free = [("view", 1, 2), ("view", 2 * high, n_view // (2 * high)), ("seq", low, n_seq // low)]
+    return [g for g in free if g[2] > 1], ("seq", 1, low), ("view", 2, high)
 
 
 def kernel(
@@ -36,7 +31,7 @@
     counts_s, gate_hbm, neigh_hbm, q_hbm, k_hbm, v_hbm, c_hbm,
     out_ref, dq_ref, dk_ref, dv_ref, gg_ref,
     gate_s, neigh_s, kv, qg, cot, stats, gacc, gbuf,
-    small_sem, load_sem, send_sem, recv_sem, g_send, g_recv,
+    small_sem, load_sem, send_sem, recv_sem, g_send, g_recv, far_sem, low_sem,
 ):
     n_view, n_seq, pairs, head_size = sizes
     tokens = kv.shape[3]
@@ -45,24 +40,34 @@
     me_seq = lax.axis_index("seq")
     core = lax.rem(me, 2)
     sibling = me + 1 - 2 * core
-    rounds = sum_rounds(n_view, n_seq)
+    free, z_lo, z_hi = sum_groups(n_view, n_seq)
 
     def view_at(offset):
         return lax.rem(me + offset + n_view, n_view)
 
-    def partner(group, step):
-        index = {"view": me, "seq": me_seq}
-        place = 0
-        for axis, stride, size in group:
-            place = place * size + lax.rem(index[axis] // stride, size)
-        other = lax.rem(place + step, group_size(group))
-        target = {}
-        rest = other
-        for axis, stride, size in reversed(group):
-            digit = lax.rem(index[axis] // stride, size)
-            target[axis] = index[axis] + (lax.rem(rest, size) - digit) * stride
-            rest = rest // size
-        return target, place, other
+    def digit_of(digit):
+        axis, stride, size = digit
+        return lax.rem((me if axis == "view" else me_seq) // stride, size)
+
+    def partner(digit, step):
+        axis, stride, size = digit
+        here = digit_of(digit)
+        there = lax.rem(here + step, size)
+        return {axis: (me if axis == "view" else me_seq) + (there - here) * stride}, there
+
+    barrier = pltpu.get_barrier_semaphore()
+    greeted = 0
+    for target in (view_at(2), view_at(-2), sibling):
+        pl.semaphore_signal(
+            barrier, inc=1, device_id={"view": target}, device_id_type=MESH
+        )
+        greeted += 1
+    for digit in free + [z_lo]:
+        for step in range(1, digit[2]):
+            pl.semaphore_signal(
+                barrier, inc=1, device_id=partner(digit, step)[0], device_id_type=MESH
+            )
+            greeted += 1
 
     def load(hbm, column, p, dst):
         return pltpu.make_async_copy(
@@ -90,20 +95,10 @@
     for copy in smalls:
         copy.start()
 
-    barrier = pltpu.get_barrier_semaphore()
-    greeted = 0
-    for offset in OFFSETS[1:]:
-        pl.semaphore_signal(
-            barrier, inc=1, device_id={"view": view_at(offset)}, device_id_type=MESH
-        )
-        greeted += 1
-    for group in rounds:
-        for step in range(1, group_size(group)):
-            pl.semaphore_signal(
-                barrier, inc=1, device_id=partner(group, step)[0], device_id_type=MESH
-            )
-            greeted += 1
     pl.semaphore_wait(barrier, greeted)
+    pl.semaphore_signal(
+        far_sem, inc=1, device_id={"view": view_at(-2)}, device_id_type=MESH
+    )
 
     def views(kind, p, slot):
         if kind is STATS:
@@ -141,9 +136,9 @@
         ).wait_recv()
 
     def pass_on(kind, p):
-        arrived(kind, p, FROM_LOW2)
-        arrived(kind, p, FROM_HIGH2)
+        arrived(kind, p, 4 - 3 * core)
         block_copy(kind, p, 3).start()
+        arrived(kind, p, 1 + 3 * core)
 
     def chip_arrived(kind, p):
         arrived(kind, p, FROM_LOW1)
@@ -153,15 +148,41 @@
         for index in range(4):
             block_copy(kind, p, index).wait_send()
 
+    window = jnp.int32(WINDOWS[0])
+    for place in range(1, len(WINDOWS)):
+        here = lax.rem(me_seq, len(WINDOWS)) == place
+        window = jnp.where(here, WINDOWS[place], window)
+
     for p in range(pairs):
         loads[p][0].wait()
         loads[p][1].wait()
-        send(KEYS, p)
+        if p < min(WINDOWS):
+            send(KEYS, p)
+        elif p < max(WINDOWS):
+
+            @pl.when(p < window)
+            def _():
+                send(KEYS, p)
+        if p == 1:
+            pl.semaphore_wait(far_sem, 1)
+            for step in range(1, z_lo[2]):
+                pl.semaphore_signal(
+                    low_sem, inc=1, device_id=partner(z_lo, step)[0], device_id_type=MESH
+                )
     for p in range(pairs):
         loads[p][2].wait()
         loads[p][3].wait()
     for copy in smalls:
         copy.wait()
+    lane = lax.broadcasted_iota(jnp.int32, (tokens, LANES), 1)
+    low_half = lane < head_size
+    last = pairs - 1
+
+    def gate_of(p):
+        return jnp.where(low_half[:1], gate_s[2 * p], gate_s[2 * p + 1])
+
+    for p in range(pairs):
+        qg[p, 0, 1] = (gate_of(p) * cot[p].astype(jnp.float32)).astype(jnp.bfloat16)
 
     bias = [jnp.float32(0.0)]
     for offset in OFFSETS[1:]:
@@ -171,8 +192,6 @@
             present = present | ((neigh_s[0, j] == view) & (counts_s[0] > j))
         bias.append(jnp.where(present, jnp.float32(0.0), jnp.float32(-jnp.inf)))
     bias_row = jnp.concatenate([jnp.full((1, tokens), b, jnp.float32) for b in bias], axis=1)
-    lane = lax.broadcasted_iota(jnp.int32, (tokens, LANES), 1)
-    low_half = lane < head_size
 
     def stacked(block):
         zero = jnp.zeros_like(block)
@@ -195,10 +214,9 @@
 
     def query_side(p):
         columns = pl.ds(pl.multiple_of(p * LANES, LANES), LANES)
-        gate_row = jnp.where(low_half[:1], gate_s[2 * p], gate_s[2 * p + 1])
+        gate_row = gate_of(p)
         cot_block = cot[p].astype(jnp.float32)
-        grad = (gate_row * cot_block).astype(jnp.bfloat16)
-        qg[p, 0, 1] = grad
+        grad = qg[p, 0, 1]
         keys = kv[p, :, 0].reshape(5 * tokens, LANES)
         values = kv[p, :, 1].reshape(5 * tokens, LANES)
         scores = dot_t(stacked(qg[p, 0, 0]), keys) * scale + bias_row
@@ -218,11 +236,6 @@
         table = jnp.where(lane == 3, delta_high, table)
         stats[p, 0] = jnp.transpose(table)[:8]
         send(STATS, p)
-
-        @pl.when(p < pairs - 1)
-        def _():
-            send(QUERIES, p)
-
         prob_grad = dot_t(stacked(grad), values)
         delta = jnp.concatenate([delta_low, delta_high], axis=0)
         score_grad = (probs * (prob_grad - delta) * scale).astype(jnp.bfloat16)
@@ -252,43 +265,81 @@
         score_grad = (probs * (prob_grad - delta) * scale).astype(jnp.bfloat16)
         dk_ref[0, :, columns] = unstacked(dot(score_grad, queries)).astype(jnp.bfloat16)
 
+    def gate_row(r, place):
+        return gbuf.at[r, place, pl.ds(0, 1)]
+
     def gate_copy(r, step):
-        target, place, _ = partner(rounds[r], step)
-        row = gbuf.at[r, place, pl.ds(0, 1)]
+        target, _ = partner(free[r], step)
+        place = digit_of(free[r])
         return pltpu.make_async_remote_copy(
-            src_ref=row,
-            dst_ref=row,
+            src_ref=gate_row(r, place),
+            dst_ref=gate_row(r, place),
             send_sem=g_send.at[r, step],
             recv_sem=g_recv.at[r, place],
             device_id=target,
             device_id_type=MESH,
         )
 
-    def gate_send(r, row):
-        gbuf[r, partner(rounds[r], 0)[1], pl.ds(0, 1)] = row
-        for step in range(1, group_size(rounds[r])):
+    def gate_arrived(r, place):
+        row = gate_row(r, place)
+        pltpu.make_async_remote_copy(
+            src_ref=row,
+            dst_ref=row,
+            send_sem=g_send.at[r, 0],
+            recv_sem=g_recv.at[r, place],
+            device_id={"view": sibling},
+            device_id_type=MESH,
+        ).wait_recv()
+
+    def gate_total(r, size):
+        total = gbuf[r, 0, pl.ds(0, 1)]
+        for i in range(1, size):
+            total = total + gbuf[r, i, pl.ds(0, 1)]
+        return total
+
+    def free_round(r, row):
+        gbuf[r, digit_of(free[r]), pl.ds(0, 1)] = row
+        for step in range(1, free[r][2]):
             gate_copy(r, step).start()
-
-    def gate_total(r):
-        for step in range(1, group_size(rounds[r])):
-            target, place, other = partner(rounds[r], step)
-            pltpu.make_async_remote_copy(
-                src_ref=gbuf.at[r, place, pl.ds(0, 1)],
-                dst_ref=gbuf.at[r, other, pl.ds(0, 1)],
-                send_sem=g_send.at[r, step],
-                recv_sem=g_recv.at[r, other],
+        for step in range(1, free[r][2]):
+            gate_arrived(r, partner(free[r], step)[1])
+        return gate_total(r, free[r][2])
+
+    z_round = len(free)
+    z_place = digit_of(z_hi) * z_lo[2] + digit_of(z_lo)
+
+    def z_partners():
+        for step_hi, distance in ((0, 0),) + Z_STEPS:
+            for step in range(z_lo[2]):
+                if distance or step:
+                    target, low = partner(z_lo, step)
+                    high = lax.rem(digit_of(z_hi) + step_hi + z_hi[2], z_hi[2])
+                    yield {"view": view_at(distance), **target}, high * z_lo[2] + low
+
+    def z_copies():
+        for index, (target, _) in enumerate(z_partners()):
+            yield pltpu.make_async_remote_copy(
+                src_ref=gate_row(z_round, z_place),
+                dst_ref=gate_row(z_round, z_place),
+                send_sem=g_send.at[z_round, index],
+                recv_sem=g_recv.at[z_round, z_place],
                 device_id=target,
                 device_id_type=MESH,
-            ).wait_recv()
-        total = gbuf[r, 0, pl.ds(0, 1)]
-        for i in range(1, group_size(rounds[r])):
-            total = total + gbuf[r, i, pl.ds(0, 1)]
-        return total
+            )
+
+    def send_later(i, base):
+        low, high = base + min(WINDOWS), base + pairs + max(WINDOWS)
+        for index in range(low, min(2 * pairs, high)):
+
+            @pl.when(i + base == index - window)
+            def _():
+                send(index // pairs, index % pairs)
 
     def first_step(i, carry):
         @pl.when(i < pairs)
         def _():
             pass_on(KEYS, i)
+            send_later(i, 0)
 
         @pl.when(i > 0)
         def _():
@@ -307,16 +358,19 @@
     spread = jnp.where(place == 2 * row, sums_low, 0.0) + jnp.where(
         place == 2 * row + 1, sums_high, 0.0
     )
-    gate_row = jnp.sum(spread, axis=0, keepdims=True)
-    for r in range(len(rounds) - 1):
-        gate_send(r, gate_row)
-        gate_row = gate_total(r)
-    gate_send(len(rounds) - 1, gate_row)
-    send(QUERIES, pairs - 1)
+    row_sums = jnp.sum(spread, axis=0, keepdims=True)
+    for r in range(len(free)):
+        row_sums = free_round(r, row_sums)
+    gbuf[z_round, z_place, pl.ds(0, 1)] = row_sums
+    if z_lo[2] > 1:
+        pl.semaphore_wait(low_sem, z_lo[2] - 1)
+    for copy in z_copies():
+        copy.start()
 
     def second_step(i, carry):
         pass_on(STATS, i)
         pass_on(QUERIES, i)
+        send_later(i, pairs)
 
         @pl.when(i > 0)
         def _():
@@ -329,17 +383,20 @@
 
         return carry
 
-    last = pairs - 1
     lax.fori_loop(0, last, second_step, 0)
     chip_arrived(STATS, last - 1)
     chip_arrived(QUERIES, last - 1)
     key_side(last - 1)
     pass_on(STATS, last)
     divisor = math.sqrt(n_view * n_seq * tokens * head_size)
-    gg_ref[...] = gate_total(len(rounds) - 1) * (1.0 / divisor)
-    for r in range(len(rounds)):
-        for step in range(1, group_size(rounds[r])):
+    for _, place in z_partners():
+        gate_arrived(z_round, place)
+    gg_ref[...] = gate_total(z_round, z_hi[2] * z_lo[2]) * (1.0 / divisor)
+    for r in range(len(free)):
+        for step in range(1, free[r][2]):
             gate_copy(r, step).wait_send()
+    for copy in z_copies():
+        copy.wait_send()
     sent(KEYS, last - 1)
     sent(STATS, last - 1)
     sent(QUERIES, last - 1)
@@ -367,8 +424,8 @@
     heads = head_gate.shape[0]
     pairs = width // LANES
     n_view, n_seq = lax.axis_size("view"), lax.axis_size("seq")
-    rounds = sum_rounds(n_view, n_seq)
-    most = max(group_size(g) for g in rounds)
+    free, z_lo, z_hi = sum_groups(n_view, n_seq)
+    rounds, most = len(free) + 1, max(z_lo[2] * z_hi[2], *(digit[2] for digit in free))
     vmem = pl.BlockSpec(memory_space=pltpu.VMEM)
     hbm = pl.BlockSpec(memory_space=pltpu.HBM)
     rows = jax.ShapeDtypeStruct(query_rows.shape, jnp.bfloat16)
@@ -388,13 +445,15 @@
             pltpu.VMEM((pairs, tokens, LANES), jnp.bfloat16),
             pltpu.VMEM((pairs, 5, 8, LANES), jnp.float32),
             pltpu.VMEM((8, LANES), jnp.float32),
-            pltpu.VMEM((len(rounds), most, 8, LANES), jnp.float32),
+            pltpu.VMEM((rounds, most, 8, LANES), jnp.float32),
             dma((2,)),
             dma((pairs, 4)),
             dma((3, pairs, 4)),
             dma((3, pairs, 5)),
-            dma((len(rounds), most)),
-            dma((len(rounds), most)),
+            dma((rounds, most)),
+            dma((rounds, most)),
+            pltpu.SemaphoreType.REGULAR,
+            pltpu.SemaphoreType.REGULAR,
         ],
         compiler_params=pltpu.CompilerParams(
             collective_id=0, has_side_effects=True, vmem_limit_bytes=40 * 1024 * 1024

time: 96.8 us -> 95 us (0.981)
  Pallas kernels: 95.4 us -> 92.9 us
    pallas_call x1, Pallas kernels: 94 us -> 91.5 us  [shards(): pl.pallas_call(functools.partial(kernel, (n_view, n_seq, pairs, width //...]
where the time goes in v3:
time: 95 us; the launch traced here: 94.2 us
  Pallas kernels  92.9 us (98%)
  between operations  1.29 us (1%)
    pallas_call x1, Pallas kernels, shards(): pl.pallas_call(functools.partial(kernel, (n_view, n_seq, pairs, width //...  91.5 us

profile of v3, /device:TPU:1, one launch (start us, length us, event | category | flops | bytes accessed | tf_op | source)
XLA Modules:
  0.0 94.2 jit_solution(8025885964824294792)
XLA Ops:
  1.3 91.5 %shard_map.110 = (bf16[1,128,768]{2,1,0:T(8,128)(2,1)S(1)}, bf16[1,128,768]{2,1,0:T(8,128)(2,1)S(1)}, bf16[1,128,768]{2,1,0:T(8,128)(2,1)S(1)}, bf16[1,128,768]{2,1,0:T(8,128)(2,1)S(1)}, f32[1,128]{1,0:T(1,128)S(1)}) custom-call(s32[1]{0:T(128)S(6)} %copy.12.counts_s, f32[12]{0:T(128)} %gate_hbm.1, s32[1,4]{1,0:T(1,128)} %neigh_hbm.1, ...), custom_call_target="tpu_custom_call" | custom-call | flops 1006632960 | bytes 3200000 | tf_op jit(solution)/shard_map/pallas_call | solution.py:434
  92.7 1.4 %shard_map.111 = (bf16[1,128,768]{2,1,0:T(8,128)(2,1)}, bf16[1,128,768]{2,1,0:T(8,128)(2,1)}, bf16[1,128,768]{2,1,0:T(8,128)(2,1)}, bf16[1,128,768]{2,1,0:T(8,128)(2,1)}, f32[12]{0:T(128)}) custom-call(bf16[1,128,768]{2,1,0:T(8,128)(2,1)S(1)} %get-tuple-element.10.out, bf16[1,128,768]{2,1,0:T(8,128)(2,1)S(1)} %get-tuple-element.11.dq, ...), custom_call_target="tpu_custom_call" | custom-call | tf_op jit(solution)/shard_map/pallas_call | solution.py:465

commit v4 on v3

--- a/solution.py
+++ b/solution.py
@@ -12,7 +12,7 @@
 LANES = 128
 OFFSETS = (0, -2, -1, 1, 2)
 FROM_LOW2, FROM_LOW1, FROM_HIGH1, FROM_HIGH2 = 1, 2, 3, 4
-WINDOWS = (5, 3, 3, 5)
+WINDOWS = (5, 3, 4, 5)
 KEYS, QUERIES, STATS = 0, 1, 2
 
 
@@ -388,24 +388,24 @@
     chip_arrived(QUERIES, last - 1)
     key_side(last - 1)
     pass_on(STATS, last)
-    divisor = math.sqrt(n_view * n_seq * tokens * head_size)
-    for _, place in z_partners():
-        gate_arrived(z_round, place)
-    gg_ref[...] = gate_total(z_round, z_hi[2] * z_lo[2]) * (1.0 / divisor)
-    for r in range(len(free)):
-        for step in range(1, free[r][2]):
-            gate_copy(r, step).wait_send()
-    for copy in z_copies():
-        copy.wait_send()
     sent(KEYS, last - 1)
     sent(STATS, last - 1)
     sent(QUERIES, last - 1)
     sent(KEYS, last)
     chip_arrived(STATS, last)
     sent(STATS, last)
+    for r in range(len(free)):
+        for step in range(1, free[r][2]):
+            gate_copy(r, step).wait_send()
     pass_on(QUERIES, last)
+    divisor = math.sqrt(n_view * n_seq * tokens * head_size)
+    for _, place in z_partners():
+        gate_arrived(z_round, place)
+    gg_ref[...] = gate_total(z_round, z_hi[2] * z_lo[2]) * (1.0 / divisor)
     chip_arrived(QUERIES, last)
     key_side(last)
+    for copy in z_copies():
+        copy.wait_send()
     sent(QUERIES, last)
 
 

time: 95 us -> 94.8 us (level)
  the two profiles are of different devices: /device:TPU:1 before, /device:TPU:65 now
where the time goes in v4:
time: 94.8 us; the launch traced here: 94.7 us
  Pallas kernels  93.4 us (99%)
  between operations  1.29 us (1%)
    pallas_call x1, Pallas kernels, shards(): pl.pallas_call(functools.partial(kernel, (n_view, n_seq, pairs, width //...  92 us

profile of v4, /device:TPU:65, one launch (start us, length us, event | category | flops | bytes accessed | tf_op | source)
XLA Modules:
  0.0 94.7 jit_solution(13076366410894780933)
XLA Ops:
  1.3 92.0 %shard_map.110 = (bf16[1,128,768]{2,1,0:T(8,128)(2,1)S(1)}, bf16[1,128,768]{2,1,0:T(8,128)(2,1)S(1)}, bf16[1,128,768]{2,1,0:T(8,128)(2,1)S(1)}, bf16[1,128,768]{2,1,0:T(8,128)(2,1)S(1)}, f32[1,128]{1,0:T(1,128)S(1)}) custom-call(s32[1]{0:T(128)S(6)} %copy.12.counts_s, f32[12]{0:T(128)} %gate_hbm.1, s32[1,4]{1,0:T(1,128)} %neigh_hbm.1, ...), custom_call_target="tpu_custom_call" | custom-call | flops 1006632960 | bytes 3200000 | tf_op jit(solution)/shard_map/pallas_call | solution.py:434
  93.3 1.4 %shard_map.111 = (bf16[1,128,768]{2,1,0:T(8,128)(2,1)}, bf16[1,128,768]{2,1,0:T(8,128)(2,1)}, bf16[1,128,768]{2,1,0:T(8,128)(2,1)}, bf16[1,128,768]{2,1,0:T(8,128)(2,1)}, f32[12]{0:T(128)}) custom-call(bf16[1,128,768]{2,1,0:T(8,128)(2,1)S(1)} %get-tuple-element.10.out, bf16[1,128,768]{2,1,0:T(8,128)(2,1)S(1)} %get-tuple-element.11.dq, ...), custom_call_target="tpu_custom_call" | custom-call | tf_op jit(solution)/shard_map/pallas_call | solution.py:465

commit v5 on v4

--- a/solution.py
+++ b/solution.py
@@ -102,7 +102,7 @@
 
     def views(kind, p, slot):
         if kind is STATS:
-            return stats.at[p, slot, pl.ds(0, 4)]
+            return stats.at[p, slot]
         return (kv if kind is KEYS else qg).at[p, slot]
 
     def block_copy(kind, p, index):
@@ -234,8 +234,12 @@
         table = jnp.where(lane == 0, log_total[:tokens], log_total[tokens:])
         table = jnp.where(lane == 2, delta_low, table)
         table = jnp.where(lane == 3, delta_high, table)
-        stats[p, 0] = jnp.transpose(table)[:8]
-        send(STATS, p)
+        stats[p // 2, 0, pl.ds(pl.multiple_of(lax.rem(p, 2) * 4, 4), 4)] = jnp.transpose(table)[:4]
+
+        @pl.when(lax.rem(p, 2) == 1)
+        def _():
+            send(STATS, p // 2)
+
         prob_grad = dot_t(stacked(grad), values)
         delta = jnp.concatenate([delta_low, delta_high], axis=0)
         score_grad = (probs * (prob_grad - delta) * scale).astype(jnp.bfloat16)
@@ -245,8 +249,9 @@
         columns = pl.ds(pl.multiple_of(p * LANES, LANES), LANES)
         queries = qg[p, :, 0].reshape(5 * tokens, LANES)
         grads = qg[p, :, 1].reshape(5 * tokens, LANES)
-        tables = [stats[p, slot] for slot in range(5)]
-        rows = jnp.concatenate(tables, axis=1)
+        tables = [stats[p // 2, slot] for slot in range(5)]
+        both_rows = jnp.concatenate(tables, axis=1)
+        rows = jnp.where(p % 2 == 0, both_rows[:4], both_rows[4:])
 
         def both(first, second):
             shape = (tokens, 5 * tokens)
@@ -368,32 +373,35 @@
         copy.start()
 
     def second_step(i, carry):
-        pass_on(STATS, i)
+        @pl.when(lax.rem(i, 2) == 0)
+        def _():
+            pass_on(STATS, i // 2)
+
         pass_on(QUERIES, i)
         send_later(i, pairs)
 
         @pl.when(i > 0)
         def _():
-            chip_arrived(STATS, i - 1)
+            @pl.when(lax.rem(i, 2) == 1)
+            def _():
+                chip_arrived(STATS, i // 2)
+
             chip_arrived(QUERIES, i - 1)
             key_side(i - 1)
             sent(KEYS, i - 1)
-            sent(STATS, i - 1)
             sent(QUERIES, i - 1)
 
         return carry
 
     lax.fori_loop(0, last, second_step, 0)
-    chip_arrived(STATS, last - 1)
+    chip_arrived(STATS, last // 2)
     chip_arrived(QUERIES, last - 1)
     key_side(last - 1)
-    pass_on(STATS, last)
     sent(KEYS, last - 1)
-    sent(STATS, last - 1)
     sent(QUERIES, last - 1)
     sent(KEYS, last)
-    chip_arrived(STATS, last)
-    sent(STATS, last)
+    for p in range(pairs // 2):
+        sent(STATS, p)
     for r in range(len(free)):
         for step in range(1, free[r][2]):
             gate_copy(r, step).wait_send()
@@ -443,7 +451,7 @@
             pltpu.VMEM((pairs, 5, 2, tokens, LANES), jnp.bfloat16),
             pltpu.VMEM((pairs, 5, 2, tokens, LANES), jnp.bfloat16),
             pltpu.VMEM((pairs, tokens, LANES), jnp.bfloat16),
-            pltpu.VMEM((pairs, 5, 8, LANES), jnp.float32),
+            pltpu.VMEM((pairs // 2, 5, 8, LANES), jnp.float32),
             pltpu.VMEM((8, LANES), jnp.float32),
             pltpu.VMEM((rounds, most, 8, LANES), jnp.float32),
             dma((2,)),

time: 94.8 us -> 93.8 us (0.989)
  the two profiles are of different devices: /device:TPU:65 before, /device:TPU:1 now
where the time goes in v5:
time: 93.8 us; the launch traced here: 92.9 us
  Pallas kernels  91.7 us (98%)
  between operations  1.29 us (1%)
    pallas_call x1, Pallas kernels, shards(): pl.pallas_call(functools.partial(kernel, (n_view, n_seq, pairs, width //...  90.2 us

profile of v5, /device:TPU:1, one launch (start us, length us, event | category | flops | bytes accessed | tf_op | source)
XLA Modules:
  0.0 92.9 jit_solution(8138069006067615790)
XLA Ops:
  1.3 90.2 %shard_map.110 = (bf16[1,128,768]{2,1,0:T(8,128)(2,1)S(1)}, bf16[1,128,768]{2,1,0:T(8,128)(2,1)S(1)}, bf16[1,128,768]{2,1,0:T(8,128)(2,1)S(1)}, bf16[1,128,768]{2,1,0:T(8,128)(2,1)S(1)}, f32[1,128]{1,0:T(1,128)S(1)}) custom-call(s32[1]{0:T(128)S(6)} %copy.12.counts_s, f32[12]{0:T(128)} %gate_hbm.1, s32[1,4]{1,0:T(1,128)} %neigh_hbm.1, ...), custom_call_target="tpu_custom_call" | custom-call | flops 1006632960 | bytes 3200000 | tf_op jit(solution)/shard_map/pallas_call | solution.py:442
  91.5 1.4 %shard_map.111 = (bf16[1,128,768]{2,1,0:T(8,128)(2,1)}, bf16[1,128,768]{2,1,0:T(8,128)(2,1)}, bf16[1,128,768]{2,1,0:T(8,128)(2,1)}, bf16[1,128,768]{2,1,0:T(8,128)(2,1)}, f32[12]{0:T(128)}) custom-call(bf16[1,128,768]{2,1,0:T(8,128)(2,1)S(1)} %get-tuple-element.10.out, bf16[1,128,768]{2,1,0:T(8,128)(2,1)S(1)} %get-tuple-element.11.dq, ...), custom_call_target="tpu_custom_call" | custom-call | tf_op jit(solution)/shard_map/pallas_call | solution.py:473
